TPU v7x, 512 devices: a whole 4x8x8 slice. The times are simulated.
512 devices in a mesh: area: 128 (over z, y, core), nrn: 4 (over x).
Axes of the slice: x: 4, y: 8, z: 8, core: 2. Of those that a mesh axis runs over, the one named last changes fastest.
Arguments:
- history: float32 [4, 65536, 128], P(None, ('area', 'nrn')), may hold values from -1 to 1
- drive: float32 [65536, 128], P(('area', 'nrn')), may hold values from -6 to 6
- leak: float32 [65536], P(('area', 'nrn')), may hold values from 0.1 to 0.9
- w_local: float32 [65536, 512], P(('area', 'nrn')), may hold values from -0.25 to 0.25
- w_long: float32 [65536, 4, 1152], P(('area', 'nrn')), may hold values from -0.1875 to 0.1875
- sender_rows: int32 [512, 128, 9], P(('area', 'nrn')), may hold values from 0 to 127
- delays: int32 [128, 128], P('area'), may hold values from 1 to 4
- area_sizes: int32 [128], P('area'), may hold values from 256 to 512, as said below
Outputs:
- rates: float32 [65536, 128], P(('area', 'nrn'))
Inputs may be any that keep to these rules, and one draw needn't show every extreme that they name: `area_sizes`: every area has at least half of its 512 slots live; some area has all of them live, some exactly half. `sender_rows`: indices may repeat.
All inputs are finite; a program needn't handle non-finite values.
Results may differ from a plain program's by a relative error of at most 0.0018.
Values may be sent and summed in bfloat16 or wider, within the bound.
A program may use at most 64 MiB of HBM per device.

v0:
```python
import jax
import jax.numpy as jnp
from jax import lax
from jax.sharding import PartitionSpec as P

STEPS = 6


def cut_along(x, dim, peers):
    lengths = x.shape
    pieces = x.reshape(*lengths[:dim], peers, lengths[dim] // peers, *lengths[dim + 1 :])
    return jnp.moveaxis(pieces, dim, 0)


def sum_at_owner(x, axis, dim):
    peers = lax.axis_size(axis)
    pieces = lax.all_to_all(cut_along(x, dim, peers), axis, 0, 0, tiled=True)
    return jnp.sum(pieces, axis=0)


def unround(values):
    return lax.optimization_barrier(values).astype(jnp.float32)


def local(history, drive, leak, w_local, w_long, sender_rows, delays, area_sizes):
    history_depth, block_rows, stimuli = history.shape
    nrn_count = lax.axis_size("nrn")
    area_count = sender_rows.shape[1]
    proj_count = sender_rows.shape[2]
    offsets = lax.axis_index("nrn") * block_rows + jnp.arange(block_rows, dtype=jnp.int32)
    active = (offsets < area_sizes[0]).astype(jnp.float32)[:, None]
    states = history * active[None]
    picked = ((delays[0] - 1)[:, None] * block_rows + sender_rows[0]).reshape(-1)
    grouped = lax.all_to_all(w_long, "nrn", split_axis=1, concat_axis=0, tiled=True).reshape(
        nrn_count * block_rows, -1
    )
    for iteration in range(STEPS):
        flat_states = states.reshape(history_depth * block_rows, stimuli)
        outgoing = flat_states[picked].astype(jnp.bfloat16).reshape(area_count, proj_count, stimuli)
        incoming = lax.all_to_all(outgoing, "area", split_axis=0, concat_axis=0, tiled=True)
        current = states[0].astype(jnp.bfloat16)
        local_all = lax.all_gather(current, "nrn", axis=0, tiled=True)
        sources = unround(incoming).reshape(-1, stimuli)
        long_term = sum_at_owner(
            jnp.dot(
                grouped,
                sources,
                precision=lax.Precision.HIGHEST,
                preferred_element_type=jnp.float32,
            ),
            "nrn",
            0,
        )
        inputs = (
            long_term
            + jnp.dot(
                w_local,
                unround(local_all),
                precision=lax.Precision.HIGHEST,
                preferred_element_type=jnp.float32,
            )
            + drive
        )
        updated = active * (states[0] + leak[:, None] * (jnp.tanh(inputs) - states[0]))
        states = jnp.concatenate([updated[None], states[:-1]], axis=0)
    return states[0]


def solution(mesh):
    placed = (
        P(None, ("area", "nrn"), None),
        P(("area", "nrn"), None),
        P(("area", "nrn")),
        P(("area", "nrn"), None),
        P(("area", "nrn"), None, None),
        P(("area", "nrn"), None, None),
        P("area", None),
        P("area"),
    )
    return jax.shard_map(
        local, mesh=mesh, in_specs=placed, out_specs=P(("area", "nrn"), None), check_vma=False
    )
```

profile of v0, /device:TPU:8, one launch (start us, length us, event | category | flops | bytes accessed | tf_op | source)
XLA Modules:
  0.0 353.5 jit_solution(10322337798542457753)
XLA Ops:
  1.7 0.8 copy.13
  2.7 1.0 broadcast_multiply_fusion
  3.8 2.5 gather_fusion
  6.3 0.9 convert_element_type.85
  7.2 17.4 %all-to-all-start = ((bf16[128,9,128]{2,1,0:T(8,128)(2,1)}), bf16[128,9,128]{2,1,0:T(8,128)(2,1)S(1)}, u32[]{:S(2)}, u32[]{:S(2)}) async-start(bf16[128,9,128]{2,1,0:T(8,128)(2,1)} %convert_element_type.85), calls=%async_computation | async-start | bytes 1048576 | tf_op jit(solution)/shard_map/all_to_all | solution.py:40
  24.6 1.6 copy.14
  26.2 18.6 %all-to-all-done = bf16[128,9,128]{2,1,0:T(8,128)(2,1)S(1)} async-done(((bf16[128,9,128]{2,1,0:T(8,128)(2,1)}), bf16[128,9,128]{2,1,0:T(8,128)(2,1)S(1)}, u32[]{:S(2)}, u32[]{:S(2)}) %all-to-all-start) | async-done | bytes 294944 | tf_op jit(solution)/shard_map/all_to_all | solution.py:40
  44.8 4.3 %all-to-all-start.1 = ((f32[128,4,1152]{2,0,1:T(8,128)}), f32[128,4,1152]{2,0,1:T(8,128)S(1)}, u32[]{:S(2)}, u32[]{:S(2)}) async-start(f32[128,4,1152]{2,0,1:T(8,128)} %copy.14), calls=%async_computation.1 | async-start | bytes 4718592 | tf_op jit(solution)/shard_map/all_to_all | solution.py:34
  49.7 0.9 reshape.130
  50.6 27.7 %all-to-all-done.1 = f32[128,4,1152]{2,0,1:T(8,128)S(1)} async-done(((f32[128,4,1152]{2,0,1:T(8,128)}), f32[128,4,1152]{2,0,1:T(8,128)S(1)}, u32[]{:S(2)}, u32[]{:S(2)}) %all-to-all-start.1) | async-done | bytes 2359328 | tf_op jit(solution)/shard_map/all_to_all | solution.py:34
  78.3 2.4 convolution_bitcast_fusion.5
  81.5 3.4 all-to-all-start.2
  84.9 13.0 %all_gather.18 = bf16[512,128]{1,0:T(8,128)(2,1)S(1)} all-gather(bf16[128,128]{1,0:T(8,128)(2,1)S(1)} %fusion.46), channel_id=1, replica_groups=mesh['area'=128,'nrn'=4] {'nrn'}, dimensions={0}, use_global_device_ids=true | all-gather | bytes 163840 | tf_op jit(solution)/shard_map/all_gather | solution.py:42
  99.0 2.9 gather_fusion.1
  102.0 27.2 %all_to_all.75 = bf16[128,9,128]{2,1,0:T(8,128)(2,1)} all-to-all(bf16[128,9,128]{2,1,0:T(8,128)(2,1)S(1)} %convert_element_type.88), channel_id=1, replica_groups=mesh['area'=128,'nrn'=4] {'area'}, dimensions={0} | all-to-all | bytes 589824 | tf_op jit(solution)/shard_map/all_to_all | solution.py:40
  129.2 1.2 reshape.134
  130.4 1.5 convolution_bitcast_fusion.4
  132.6 3.4 all-to-all-start.4
  136.0 13.8 %all_gather.19 = bf16[512,128]{1,0:T(8,128)(2,1)S(1)} all-gather(bf16[128,128]{1,0:T(8,128)(2,1)S(1)} %get-tuple-element.5), channel_id=1, replica_groups=mesh['area'=128,'nrn'=4] {'nrn'}, dimensions={0}, use_global_device_ids=true | all-gather | bytes 163840 | tf_op jit(solution)/shard_map/all_gather | solution.py:42
  150.9 2.9 gather_fusion.2
  154.0 25.9 %all_to_all.76 = bf16[128,9,128]{2,1,0:T(8,128)(2,1)} all-to-all(bf16[128,9,128]{2,1,0:T(8,128)(2,1)S(1)} %convert_element_type.91), channel_id=1, replica_groups=mesh['area'=128,'nrn'=4] {'area'}, dimensions={0} | all-to-all | bytes 589824 | tf_op jit(solution)/shard_map/all_to_all | solution.py:40
  179.9 1.2 reshape.137
  181.1 1.5 convolution_bitcast_fusion.3
  182.6 0.7 copy.56
  183.3 3.4 all-to-all-start.6
  186.7 13.8 %all_gather.20 = bf16[512,128]{1,0:T(8,128)(2,1)S(1)} all-gather(bf16[128,128]{1,0:T(8,128)(2,1)S(1)} %get-tuple-element.7), channel_id=1, replica_groups=mesh['area'=128,'nrn'=4] {'nrn'}, dimensions={0}, use_global_device_ids=true | all-gather | bytes 163840 | tf_op jit(solution)/shard_map/all_gather | solution.py:42
  201.6 2.9 gather_fusion.3
  204.6 25.9 %all_to_all.77 = bf16[128,9,128]{2,1,0:T(8,128)(2,1)} all-to-all(bf16[128,9,128]{2,1,0:T(8,128)(2,1)S(1)} %convert_element_type.94), channel_id=1, replica_groups=mesh['area'=128,'nrn'=4] {'area'}, dimensions={0} | all-to-all | bytes 589824 | tf_op jit(solution)/shard_map/all_to_all | solution.py:40
  230.6 1.2 reshape.140
  231.8 1.5 convolution_bitcast_fusion.2
  233.3 0.7 copy.55
  234.0 3.4 all-to-all-start.8
  237.4 13.8 %all_gather.21 = bf16[512,128]{1,0:T(8,128)(2,1)S(1)} all-gather(bf16[128,128]{1,0:T(8,128)(2,1)S(1)} %get-tuple-element.9), channel_id=1, replica_groups=mesh['area'=128,'nrn'=4] {'nrn'}, dimensions={0}, use_global_device_ids=true | all-gather | bytes 163840 | tf_op jit(solution)/shard_map/all_gather | solution.py:42
  252.3 2.9 gather_fusion.4
  255.3 25.9 %all_to_all.78 = bf16[128,9,128]{2,1,0:T(8,128)(2,1)} all-to-all(bf16[128,9,128]{2,1,0:T(8,128)(2,1)S(1)} %convert_element_type.97), channel_id=1, replica_groups=mesh['area'=128,'nrn'=4] {'area'}, dimensions={0} | all-to-all | bytes 589824 | tf_op jit(solution)/shard_map/all_to_all | solution.py:40
  281.3 1.2 reshape.143
  282.5 1.5 convolution_bitcast_fusion.1
  283.9 0.7 copy.54
  284.7 3.4 all-to-all-start.10
  288.1 13.7 %all_gather.22 = bf16[512,128]{1,0:T(8,128)(2,1)S(1)} all-gather(bf16[128,128]{1,0:T(8,128)(2,1)S(1)} %get-tuple-element.11), channel_id=1, replica_groups=mesh['area'=128,'nrn'=4] {'nrn'}, dimensions={0}, use_global_device_ids=true | all-gather | bytes 163840 | tf_op jit(solution)/shard_map/all_gather | solution.py:42
  302.9 2.9 gather_fusion.5
  305.9 25.9 %all_to_all.79 = bf16[128,9,128]{2,1,0:T(8,128)(2,1)} all-to-all(bf16[128,9,128]{2,1,0:T(8,128)(2,1)S(1)} %convert_element_type.100), channel_id=1, replica_groups=mesh['area'=128,'nrn'=4] {'area'}, dimensions={0} | all-to-all | bytes 589824 | tf_op jit(solution)/shard_map/all_to_all | solution.py:40
  331.8 1.2 reshape.146
  333.0 1.5 convolution_bitcast_fusion
  334.5 0.7 copy.53
  335.2 3.4 all-to-all-start.12
  338.6 13.8 %all_gather.23 = bf16[512,128]{1,0:T(8,128)(2,1)S(1)} all-gather(bf16[128,128]{1,0:T(8,128)(2,1)S(1)} %get-tuple-element.13), channel_id=1, replica_groups=mesh['area'=128,'nrn'=4] {'nrn'}, dimensions={0}, use_global_device_ids=true | all-gather | bytes 163840 | tf_op jit(solution)/shard_map/all_gather | solution.py:42
  352.6 0.9 fusion.41
  (92 shorter events, 9.1 us)
Async XLA Ops:
  0.0 98.0 %copy-start = (f32[128,512]{1,0:T(8,128)S(1)}, f32[128,512]{1,0:T(8,128)}, u32[]{:S(2)}) copy-start(f32[128,512]{1,0:T(8,128)} %param.11) | copy-start | bytes 786436
  3.8 20.8 %copy-start.1 = (f32[128,4,1152]{2,1,0:T(4,128)S(1)}, f32[128,4,1152]{2,1,0:T(4,128)}, u32[]{:S(2)}) copy-start(f32[128,4,1152]{2,1,0:T(4,128)} %param.12) | copy-start | bytes 7077892
  7.2 37.6 %all-to-all-start = ((bf16[128,9,128]{2,1,0:T(8,128)(2,1)}), bf16[128,9,128]{2,1,0:T(8,128)(2,1)S(1)}, u32[]{:S(2)}, u32[]{:S(2)}) async-start(bf16[128,9,128]{2,1,0:T(8,128)(2,1)} %convert_element_type.85), calls=%async_computation | async-start | bytes 1048576 | tf_op jit(solution)/shard_map/all_to_all | solution.py:40
  44.8 33.5 %all-to-all-start.1 = ((f32[128,4,1152]{2,0,1:T(8,128)}), f32[128,4,1152]{2,0,1:T(8,128)S(1)}, u32[]{:S(2)}, u32[]{:S(2)}) async-start(f32[128,4,1152]{2,0,1:T(8,128)} %copy.14), calls=%async_computation.1 | async-start | bytes 4718592 | tf_op jit(solution)/shard_map/all_to_all | solution.py:34
  50.6 47.4 %copy-start.2 = (f32[128,128]{1,0:T(8,128)S(1)}, f32[128,128]{1,0:T(8,128)}, u32[]{:S(2)}) copy-start(f32[128,128]{1,0:T(8,128)} %param.9) | copy-start | bytes 196612
  50.6 47.4 %copy-start.21 = (f32[128]{0:T(128)S(1)}, f32[128]{0:T(128)}, u32[]{:S(2)}) copy-start(f32[128]{0:T(128)} %param.10) | copy-start | bytes 1540
  78.3 20.0 %copy-start.11 = (bf16[3,128,128]{2,1,0:T(8,128)(2,1)S(1)}, bf16[3,128,128]{2,1,0:T(8,128)(2,1)}, u32[]{:S(2)}) copy-start(bf16[3,128,128]{2,1,0:T(8,128)(2,1)} %slice.39) | copy-start | bytes 294916
  81.5 16.4 %all-to-all-start.2 = ((f32[4,128,128]{1,2,0:T(8,128)}), f32[4,128,128]{1,2,0:T(8,128)S(1)}, u32[]{:S(2)}, u32[]{:S(2)}) async-start(f32[4,128,128]{1,2,0:T(8,128)} %bitcast.180), calls=%async_computation.2 | async-start | bytes 524288 | tf_op jit(solution)/shard_map/all_to_all | solution.py:17
  98.3 0.6 copy-start.3
  129.2 20.6 %copy-start.4 = (f32[128,128]{1,0:T(8,128)S(1)}, f32[128,128]{1,0:T(8,128)}, u32[]{:S(2)}) copy-start(f32[128,128]{1,0:T(8,128)} %copy-done.3) | copy-start | bytes 196612
  129.2 20.6 %copy-start.12 = (bf16[3,128,128]{2,1,0:T(8,128)(2,1)S(1)}, bf16[3,128,128]{2,1,0:T(8,128)(2,1)}, u32[]{:S(2)}) copy-start(bf16[3,128,128]{2,1,0:T(8,128)(2,1)} %slice.39) | copy-start | bytes 294916
  132.6 17.3 %all-to-all-start.4 = ((f32[4,128,128]{1,2,0:T(8,128)}), f32[4,128,128]{1,2,0:T(8,128)S(1)}, u32[]{:S(2)}, u32[]{:S(2)}) async-start(f32[4,128,128]{1,2,0:T(8,128)} %bitcast.179), calls=%async_computation.4 | async-start | bytes 524288 | tf_op jit(solution)/shard_map/all_to_all | solution.py:17
  149.8 0.6 copy-start.13
  150.3 0.6 copy-start.5
  179.9 20.6 %copy-start.6 = (f32[128,128]{1,0:T(8,128)S(1)}, f32[128,128]{1,0:T(8,128)}, u32[]{:S(2)}) copy-start(f32[128,128]{1,0:T(8,128)} %copy-done.5) | copy-start | bytes 196612
  179.9 20.6 %copy-start.14 = (bf16[3,128,128]{2,1,0:T(8,128)(2,1)S(1)}, bf16[3,128,128]{2,1,0:T(8,128)(2,1)}, u32[]{:S(2)}) copy-start(bf16[3,128,128]{2,1,0:T(8,128)(2,1)} %copy-done.13) | copy-start | bytes 294916
  183.3 17.2 %all-to-all-start.6 = ((f32[4,128,128]{1,2,0:T(8,128)}), f32[4,128,128]{1,2,0:T(8,128)S(1)}, u32[]{:S(2)}, u32[]{:S(2)}) async-start(f32[4,128,128]{1,2,0:T(8,128)} %bitcast.178), calls=%async_computation.6 | async-start | bytes 524288 | tf_op jit(solution)/shard_map/all_to_all | solution.py:17
  200.5 0.6 copy-start.15
  200.9 0.6 copy-start.7
  230.6 20.6 %copy-start.8 = (f32[128,128]{1,0:T(8,128)S(1)}, f32[128,128]{1,0:T(8,128)}, u32[]{:S(2)}) copy-start(f32[128,128]{1,0:T(8,128)} %copy-done.7) | copy-start | bytes 196612
  230.6 20.6 %copy-start.16 = (bf16[3,128,128]{2,1,0:T(8,128)(2,1)S(1)}, bf16[3,128,128]{2,1,0:T(8,128)(2,1)}, u32[]{:S(2)}) copy-start(bf16[3,128,128]{2,1,0:T(8,128)(2,1)} %copy-done.15) | copy-start | bytes 294916
  234.0 17.2 %all-to-all-start.8 = ((f32[4,128,128]{1,2,0:T(8,128)}), f32[4,128,128]{1,2,0:T(8,128)S(1)}, u32[]{:S(2)}, u32[]{:S(2)}) async-start(f32[4,128,128]{1,2,0:T(8,128)} %bitcast.177), calls=%async_computation.8 | async-start | bytes 524288 | tf_op jit(solution)/shard_map/all_to_all | solution.py:17
  251.2 0.6 copy-start.17
  251.6 0.6 copy-start.9
  281.3 20.5 %copy-start.10 = (f32[128,128]{1,0:T(8,128)S(1)}, f32[128,128]{1,0:T(8,128)}, u32[]{:S(2)}) copy-start(f32[128,128]{1,0:T(8,128)} %copy-done.9) | copy-start | bytes 196612
  281.3 20.5 %copy-start.18 = (bf16[3,128,128]{2,1,0:T(8,128)(2,1)S(1)}, bf16[3,128,128]{2,1,0:T(8,128)(2,1)}, u32[]{:S(2)}) copy-start(bf16[3,128,128]{2,1,0:T(8,128)(2,1)} %copy-done.17) | copy-start | bytes 294916
  284.7 17.2 %all-to-all-start.10 = ((f32[4,128,128]{1,2,0:T(8,128)}), f32[4,128,128]{1,2,0:T(8,128)S(1)}, u32[]{:S(2)}, u32[]{:S(2)}) async-start(f32[4,128,128]{1,2,0:T(8,128)} %bitcast.176), calls=%async_computation.10 | async-start | bytes 524288 | tf_op jit(solution)/shard_map/all_to_all | solution.py:17
  302.2 0.6 copy-start.19
  333.0 19.5 %copy-start.20 = (f32[128,128]{1,0:T(8,128)S(1)}, f32[128,128]{1,0:T(8,128)}, u32[]{:S(2)}) copy-start(f32[128,128]{1,0:T(8,128)} %copy-done.19) | copy-start | bytes 196612
  335.2 17.2 %all-to-all-start.12 = ((f32[4,128,128]{1,2,0:T(8,128)}), f32[4,128,128]{1,2,0:T(8,128)S(1)}, u32[]{:S(2)}, u32[]{:S(2)}) async-start(f32[4,128,128]{1,2,0:T(8,128)} %bitcast.175), calls=%async_computation.12 | async-start | bytes 524288 | tf_op jit(solution)/shard_map/all_to_all | solution.py:17
where the time goes:
time: 355 us; the launch traced here: 353 us
  blocking collectives  213 us (60%)
  waiting for transfers between devices  46.3 us (13%)
  starting transfers between devices  42.1 us (12%)
  local copies, waits for them, and re-layouts  37 us (10%)
  matrix products  12 us (3%)
    all_to_all x5, blocking collectives, local(): lax.all_to_all(outgoing, 'area', split_axis=0, concat_axis=0, tiled=True)  131 us
    all_gather x6, blocking collectives, local(): local_all = lax.all_gather(current, 'nrn', axis=0, tiled=True)  81.9 us
    all_to_all x1, waiting for transfers between devices, local(): lax.all_to_all(w_long, 'nrn', split_axis=1, concat_axis=0, tiled=True)  27.7 us
    all_to_all x6, starting transfers between devices, sum_at_owner(): pieces = lax.all_to_all(cut_along(x, dim, peers), axis, 0, 0, tiled=True)  20.4 us
    all_to_all x1, waiting for transfers between devices, local(): lax.all_to_all(outgoing, 'area', split_axis=0, concat_axis=0, tiled=True)  18.6 us
    all_to_all x1, starting transfers between devices, local(): lax.all_to_all(outgoing, 'area', split_axis=0, concat_axis=0, tiled=True)  17.4 us
    gather x6, local copies, waits for them, and re-layouts, local(): flat_states[picked].astype(jnp.bfloat16)  17.1 us
    dot_general x6, matrix products, local(): jnp.dot(grouped, sources, precision=lax.Precision.HIGHEST, preferred_elem...  9.74 us
  transfers between devices with their start and end apart: 8, of which 2 were waited for; matrix products, arithmetic and copies ran while one was open for 1% of the time, Pallas kernels for 0%

commit v1 on v0

--- a/solution.py
+++ b/solution.py
@@ -4,6 +4,9 @@
 from jax.sharding import PartitionSpec as P
 
 STEPS = 6
+set_the_ranges = lambda my_data, mesh_name: jnp.concatenate(
+    lax.all_to_all(jnp.stack([my_data] * lax.axis_size(mesh_name), axis=0), mesh_name, 0, 0), axis=0
+)
 
 
 def cut_along(x, dim, peers):
@@ -39,7 +42,7 @@
         outgoing = flat_states[picked].astype(jnp.bfloat16).reshape(area_count, proj_count, stimuli)
         incoming = lax.all_to_all(outgoing, "area", split_axis=0, concat_axis=0, tiled=True)
         current = states[0].astype(jnp.bfloat16)
-        local_all = lax.all_gather(current, "nrn", axis=0, tiled=True)
+        local_all = set_the_ranges(current, "nrn")
         sources = unround(incoming).reshape(-1, stimuli)
         long_term = sum_at_owner(
             jnp.dot(

time: 355 us -> 369 us (1.039)
  the two profiles are of different devices: /device:TPU:8 before, /device:TPU:1 now
where the time goes in v1:
time: 369 us; the launch traced here: 367 us
  blocking collectives  140 us (38%)
  waiting for transfers between devices  102 us (28%)
  starting transfers between devices  66.1 us (18%)
  local copies, waits for them, and re-layouts  39 us (11%)
  matrix products  16.5 us (4%)
    all_to_all x5, blocking collectives, local(): lax.all_to_all(outgoing, 'area', split_axis=0, concat_axis=0, tiled=True)  140 us
    all_to_all x6, waiting for transfers between devices, sum_at_owner(): pieces = lax.all_to_all(cut_along(x, dim, peers), axis, 0, 0, tiled=True)  35.1 us
    all_to_all x1, waiting for transfers between devices, local(): lax.all_to_all(w_long, 'nrn', split_axis=1, concat_axis=0, tiled=True)  28.5 us
    all_to_all x6, starting transfers between devices, lax.all_to_all(jnp.stack([my_data] * lax.axis_size(mesh_name), axis=0), m...  23.1 us
    all_to_all x6, starting transfers between devices, sum_at_owner(): pieces = lax.all_to_all(cut_along(x, dim, peers), axis, 0, 0, tiled=True)  20.6 us
    all_to_all x6, waiting for transfers between devices, lax.all_to_all(jnp.stack([my_data] * lax.axis_size(mesh_name), axis=0), m...  19.1 us
    all_to_all x1, waiting for transfers between devices, local(): lax.all_to_all(outgoing, 'area', split_axis=0, concat_axis=0, tiled=True)  19 us
    all_to_all x1, starting transfers between devices, local(): lax.all_to_all(outgoing, 'area', split_axis=0, concat_axis=0, tiled=True)  18.4 us
  transfers between devices with their start and end apart: 14, of which 14 were waited for; matrix products, arithmetic and copies ran while one was open for 5% of the time, Pallas kernels for 0%

profile of v1, /device:TPU:1, one launch (start us, length us, event | category | flops | bytes accessed | tf_op | source)
XLA Modules:
  0.0 366.6 jit_solution(5924570959360936856)
XLA Ops:
  3.8 2.5 gather_fusion
  7.2 18.4 %all-to-all-start = ((bf16[128,9,128]{2,1,0:T(8,128)(2,1)}), bf16[128,9,128]{2,1,0:T(8,128)(2,1)S(1)}, u32[]{:S(2)}, u32[]{:S(2)}) async-start(bf16[128,9,128]{2,1,0:T(8,128)(2,1)} %convert_element_type.86), calls=%async_computation | async-start | bytes 1048576 | tf_op jit(solution)/shard_map/all_to_all | solution.py:43
  25.7 1.6 copy.14
  27.2 19.0 %all-to-all-done = bf16[128,9,128]{2,1,0:T(8,128)(2,1)S(1)} async-done(((bf16[128,9,128]{2,1,0:T(8,128)(2,1)}), bf16[128,9,128]{2,1,0:T(8,128)(2,1)S(1)}, u32[]{:S(2)}, u32[]{:S(2)}) %all-to-all-start) | async-done | bytes 294944 | tf_op jit(solution)/shard_map/all_to_all | solution.py:43
  46.2 4.0 %all-to-all-start.1 = ((f32[128,4,1152]{2,0,1:T(8,128)}), f32[128,4,1152]{2,0,1:T(8,128)S(1)}, u32[]{:S(2)}, u32[]{:S(2)}) async-start(f32[128,4,1152]{2,0,1:T(8,128)} %copy.14), calls=%async_computation.1 | async-start | bytes 4718592 | tf_op jit(solution)/shard_map/all_to_all | solution.py:37
  51.1 28.5 %all-to-all-done.1 = f32[128,4,1152]{2,0,1:T(8,128)S(1)} async-done(((f32[128,4,1152]{2,0,1:T(8,128)}), f32[128,4,1152]{2,0,1:T(8,128)S(1)}, u32[]{:S(2)}, u32[]{:S(2)}) %all-to-all-start.1) | async-done | bytes 2359328 | tf_op jit(solution)/shard_map/all_to_all | solution.py:37
  80.3 3.3 all-to-all-start.3
  83.6 2.4 convolution_bitcast_fusion.5
  86.8 1.6 all-to-all-done.3
  88.4 3.4 all-to-all-start.2
  91.8 5.5 %all-to-all-done.2 = f32[4,128,128]{1,2,0:T(8,128)S(1)} async-done(((f32[4,128,128]{1,2,0:T(8,128)}), f32[4,128,128]{1,2,0:T(8,128)S(1)}, u32[]{:S(2)}, u32[]{:S(2)}) %all-to-all-start.2) | async-done | bytes 262176 | tf_op jit(solution)/shard_map/all_to_all | solution.py:20
  98.4 2.9 gather_fusion.1
  102.2 29.1 %all_to_all.105 = bf16[128,9,128]{2,1,0:T(8,128)(2,1)S(1)} all-to-all(bf16[128,9,128]{2,1,0:T(8,128)(2,1)} %convert_element_type.89), channel_id=1, replica_groups=mesh['area'=128,'nrn'=4] {'area'}, dimensions={0} | all-to-all | bytes 589824 | tf_op jit(solution)/shard_map/all_to_all | solution.py:43
  132.0 3.9 %all-to-all-start.6 = ((bf16[4,128,128]{2,1,0:T(8,128)(2,1)}), bf16[4,128,128]{2,1,0:T(8,128)(2,1)}, u32[]{:S(2)}, u32[]{:S(2)}) async-start(bf16[4,128,128]{2,1,0:T(8,128)(2,1)} %stack.16), calls=%async_computation.6 | async-start | bytes 262144 | tf_op jit(solution)/shard_map/all_to_all | solution.py:8
  136.1 1.5 convolution_bitcast_fusion.4
  138.3 3.5 all-to-all-done.6
  141.8 3.4 all-to-all-start.5
  145.2 6.0 %all-to-all-done.5 = f32[4,128,128]{1,2,0:T(8,128)S(1)} async-done(((f32[4,128,128]{1,2,0:T(8,128)}), f32[4,128,128]{1,2,0:T(8,128)S(1)}, u32[]{:S(2)}, u32[]{:S(2)}) %all-to-all-start.5) | async-done | bytes 262176 | tf_op jit(solution)/shard_map/all_to_all | solution.py:20
  151.3 1.2 fusion.49
  153.1 2.9 gather_fusion.2
  157.0 27.8 %all_to_all.106 = bf16[128,9,128]{2,1,0:T(8,128)(2,1)S(1)} all-to-all(bf16[128,9,128]{2,1,0:T(8,128)(2,1)} %convert_element_type.92), channel_id=1, replica_groups=mesh['area'=128,'nrn'=4] {'area'}, dimensions={0} | all-to-all | bytes 589824 | tf_op jit(solution)/shard_map/all_to_all | solution.py:43
  185.5 3.9 %all-to-all-start.9 = ((bf16[4,128,128]{2,1,0:T(8,128)(2,1)}), bf16[4,128,128]{2,1,0:T(8,128)(2,1)}, u32[]{:S(2)}, u32[]{:S(2)}) async-start(bf16[4,128,128]{2,1,0:T(8,128)(2,1)} %stack.17), calls=%async_computation.9 | async-start | bytes 262144 | tf_op jit(solution)/shard_map/all_to_all | solution.py:8
  189.6 1.5 convolution_bitcast_fusion.3
  191.8 3.5 all-to-all-done.9
  195.3 3.4 all-to-all-start.8
  198.7 6.0 %all-to-all-done.8 = f32[4,128,128]{1,2,0:T(8,128)S(1)} async-done(((f32[4,128,128]{1,2,0:T(8,128)}), f32[4,128,128]{1,2,0:T(8,128)S(1)}, u32[]{:S(2)}, u32[]{:S(2)}) %all-to-all-start.8) | async-done | bytes 262176 | tf_op jit(solution)/shard_map/all_to_all | solution.py:20
  206.6 2.9 gather_fusion.3
  210.5 27.7 %all_to_all.107 = bf16[128,9,128]{2,1,0:T(8,128)(2,1)S(1)} all-to-all(bf16[128,9,128]{2,1,0:T(8,128)(2,1)} %convert_element_type.95), channel_id=1, replica_groups=mesh['area'=128,'nrn'=4] {'area'}, dimensions={0} | all-to-all | bytes 589824 | tf_op jit(solution)/shard_map/all_to_all | solution.py:43
  238.8 3.9 %all-to-all-start.12 = ((bf16[4,128,128]{2,1,0:T(8,128)(2,1)}), bf16[4,128,128]{2,1,0:T(8,128)(2,1)}, u32[]{:S(2)}, u32[]{:S(2)}) async-start(bf16[4,128,128]{2,1,0:T(8,128)(2,1)} %stack.18), calls=%async_computation.12 | async-start | bytes 262144 | tf_op jit(solution)/shard_map/all_to_all | solution.py:8
  243.0 1.5 convolution_bitcast_fusion.2
  245.1 3.5 all-to-all-done.12
  248.6 3.4 all-to-all-start.11
  252.1 6.0 %all-to-all-done.11 = f32[4,128,128]{1,2,0:T(8,128)S(1)} async-done(((f32[4,128,128]{1,2,0:T(8,128)}), f32[4,128,128]{1,2,0:T(8,128)S(1)}, u32[]{:S(2)}, u32[]{:S(2)}) %all-to-all-start.11) | async-done | bytes 262176 | tf_op jit(solution)/shard_map/all_to_all | solution.py:20
  260.0 2.9 gather_fusion.4
  263.8 27.7 %all_to_all.108 = bf16[128,9,128]{2,1,0:T(8,128)(2,1)S(1)} all-to-all(bf16[128,9,128]{2,1,0:T(8,128)(2,1)} %convert_element_type.98), channel_id=1, replica_groups=mesh['area'=128,'nrn'=4] {'area'}, dimensions={0} | all-to-all | bytes 589824 | tf_op jit(solution)/shard_map/all_to_all | solution.py:43
  292.2 3.9 %all-to-all-start.15 = ((bf16[4,128,128]{2,1,0:T(8,128)(2,1)}), bf16[4,128,128]{2,1,0:T(8,128)(2,1)}, u32[]{:S(2)}, u32[]{:S(2)}) async-start(bf16[4,128,128]{2,1,0:T(8,128)(2,1)} %stack.19), calls=%async_computation.15 | async-start | bytes 262144 | tf_op jit(solution)/shard_map/all_to_all | solution.py:8
  296.3 1.5 convolution_bitcast_fusion.1
  298.5 3.5 all-to-all-done.15
  301.9 3.6 all-to-all-start.14
  305.6 5.7 %all-to-all-done.14 = f32[4,128,128]{1,2,0:T(8,128)S(1)} async-done(((f32[4,128,128]{1,2,0:T(8,128)}), f32[4,128,128]{1,2,0:T(8,128)S(1)}, u32[]{:S(2)}, u32[]{:S(2)}) %all-to-all-start.14) | async-done | bytes 262176 | tf_op jit(solution)/shard_map/all_to_all | solution.py:20
  313.3 2.9 gather_fusion.5
  317.1 27.7 %all_to_all.109 = bf16[128,9,128]{2,1,0:T(8,128)(2,1)S(1)} all-to-all(bf16[128,9,128]{2,1,0:T(8,128)(2,1)} %convert_element_type.101), channel_id=1, replica_groups=mesh['area'=128,'nrn'=4] {'area'}, dimensions={0} | all-to-all | bytes 589824 | tf_op jit(solution)/shard_map/all_to_all | solution.py:43
  345.5 3.9 %all-to-all-start.18 = ((bf16[4,128,128]{2,1,0:T(8,128)(2,1)}), bf16[4,128,128]{2,1,0:T(8,128)(2,1)}, u32[]{:S(2)}, u32[]{:S(2)}) async-start(bf16[4,128,128]{2,1,0:T(8,128)(2,1)} %stack.20), calls=%async_computation.18 | async-start | bytes 262144 | tf_op jit(solution)/shard_map/all_to_all | solution.py:8
  349.6 1.5 convolution_bitcast_fusion
  351.8 3.5 all-to-all-done.18
  355.3 3.4 all-to-all-start.17
  358.7 6.0 %all-to-all-done.17 = f32[4,128,128]{1,2,0:T(8,128)S(1)} async-done(((f32[4,128,128]{1,2,0:T(8,128)}), f32[4,128,128]{1,2,0:T(8,128)S(1)}, u32[]{:S(2)}, u32[]{:S(2)}) %all-to-all-start.17) | async-done | bytes 262176 | tf_op jit(solution)/shard_map/all_to_all | solution.py:20
  364.8 1.8 fusion.41
  (104 shorter events, 26.1 us)
Async XLA Ops:
  0.0 97.4 %copy-start = (f32[128,512]{1,0:T(8,128)S(1)}, f32[128,512]{1,0:T(8,128)}, u32[]{:S(2)}) copy-start(f32[128,512]{1,0:T(8,128)} %param.11) | copy-start | bytes 786436
  3.8 21.9 %copy-start.1 = (f32[128,4,1152]{2,1,0:T(4,128)S(1)}, f32[128,4,1152]{2,1,0:T(4,128)}, u32[]{:S(2)}) copy-start(f32[128,4,1152]{2,1,0:T(4,128)} %param.12) | copy-start | bytes 7077892
  7.2 39.0 %all-to-all-start = ((bf16[128,9,128]{2,1,0:T(8,128)(2,1)}), bf16[128,9,128]{2,1,0:T(8,128)(2,1)S(1)}, u32[]{:S(2)}, u32[]{:S(2)}) async-start(bf16[128,9,128]{2,1,0:T(8,128)(2,1)} %convert_element_type.86), calls=%async_computation | async-start | bytes 1048576 | tf_op jit(solution)/shard_map/all_to_all | solution.py:43
  46.2 33.4 %all-to-all-start.1 = ((f32[128,4,1152]{2,0,1:T(8,128)}), f32[128,4,1152]{2,0,1:T(8,128)S(1)}, u32[]{:S(2)}, u32[]{:S(2)}) async-start(f32[128,4,1152]{2,0,1:T(8,128)} %copy.14), calls=%async_computation.1 | async-start | bytes 4718592 | tf_op jit(solution)/shard_map/all_to_all | solution.py:37
  80.3 8.1 %all-to-all-start.3 = ((bf16[4,128,128]{2,1,0:T(8,128)(2,1)}), bf16[4,128,128]{2,1,0:T(8,128)(2,1)S(1)}, u32[]{:S(2)}, u32[]{:S(2)}) async-start(bf16[4,128,128]{2,1,0:T(8,128)(2,1)} %stack.15), calls=%async_computation.3 | async-start | bytes 262144 | tf_op jit(solution)/shard_map/all_to_all | solution.py:8
  83.6 13.8 %copy-start.2 = (f32[128,128]{1,0:T(8,128)S(1)}, f32[128,128]{1,0:T(8,128)}, u32[]{:S(2)}) copy-start(f32[128,128]{1,0:T(8,128)} %param.9) | copy-start | bytes 196612
  83.6 13.8 %copy-start.21 = (f32[128]{0:T(128)S(1)}, f32[128]{0:T(128)}, u32[]{:S(2)}) copy-start(f32[128]{0:T(128)} %param.10) | copy-start | bytes 1540
  88.4 8.9 %all-to-all-start.2 = ((f32[4,128,128]{1,2,0:T(8,128)}), f32[4,128,128]{1,2,0:T(8,128)S(1)}, u32[]{:S(2)}, u32[]{:S(2)}) async-start(f32[4,128,128]{1,2,0:T(8,128)} %bitcast.184), calls=%async_computation.2 | async-start | bytes 524288 | tf_op jit(solution)/shard_map/all_to_all | solution.py:20
  91.8 10.4 %copy-start.11 = (bf16[3,128,128]{2,1,0:T(8,128)(2,1)}, bf16[3,128,128]{2,1,0:T(8,128)(2,1)S(1)}, u32[]{:S(2)}) copy-start(bf16[3,128,128]{2,1,0:T(8,128)(2,1)S(1)} %slice.39) | copy-start | bytes 294916
  97.7 0.6 copy-start.3
  132.0 9.8 %all-to-all-start.6 = ((bf16[4,128,128]{2,1,0:T(8,128)(2,1)}), bf16[4,128,128]{2,1,0:T(8,128)(2,1)}, u32[]{:S(2)}, u32[]{:S(2)}) async-start(bf16[4,128,128]{2,1,0:T(8,128)(2,1)} %stack.16), calls=%async_computation.6 | async-start | bytes 262144 | tf_op jit(solution)/shard_map/all_to_all | solution.py:8
  136.1 9.1 %copy-start.4 = (f32[128,128]{1,0:T(8,128)S(1)}, f32[128,128]{1,0:T(8,128)}, u32[]{:S(2)}) copy-start(f32[128,128]{1,0:T(8,128)} %copy-done.3) | copy-start | bytes 196612
  136.1 9.1 %copy-start.12 = (bf16[3,128,128]{2,1,0:T(8,128)(2,1)S(1)}, bf16[3,128,128]{2,1,0:T(8,128)(2,1)}, u32[]{:S(2)}) copy-start(bf16[3,128,128]{2,1,0:T(8,128)(2,1)} %copy-done.11) | copy-start | bytes 294916
  141.8 9.4 %all-to-all-start.5 = ((f32[4,128,128]{1,2,0:T(8,128)}), f32[4,128,128]{1,2,0:T(8,128)S(1)}, u32[]{:S(2)}, u32[]{:S(2)}) async-start(f32[4,128,128]{1,2,0:T(8,128)} %bitcast.183), calls=%async_computation.5 | async-start | bytes 524288 | tf_op jit(solution)/shard_map/all_to_all | solution.py:20
  145.2 10.8 %copy-start.13 = (bf16[3,128,128]{2,1,0:T(8,128)(2,1)}, bf16[3,128,128]{2,1,0:T(8,128)(2,1)S(1)}, u32[]{:S(2)}) copy-start(bf16[3,128,128]{2,1,0:T(8,128)(2,1)S(1)} %fusion.45) | copy-start | bytes 294916
  152.5 0.6 copy-start.5
  185.5 9.8 %all-to-all-start.9 = ((bf16[4,128,128]{2,1,0:T(8,128)(2,1)}), bf16[4,128,128]{2,1,0:T(8,128)(2,1)}, u32[]{:S(2)}, u32[]{:S(2)}) async-start(bf16[4,128,128]{2,1,0:T(8,128)(2,1)} %stack.17), calls=%async_computation.9 | async-start | bytes 262144 | tf_op jit(solution)/shard_map/all_to_all | solution.py:8
  189.6 9.1 %copy-start.6 = (f32[128,128]{1,0:T(8,128)S(1)}, f32[128,128]{1,0:T(8,128)}, u32[]{:S(2)}) copy-start(f32[128,128]{1,0:T(8,128)} %copy-done.5) | copy-start | bytes 196612
  189.6 9.1 %copy-start.14 = (bf16[3,128,128]{2,1,0:T(8,128)(2,1)S(1)}, bf16[3,128,128]{2,1,0:T(8,128)(2,1)}, u32[]{:S(2)}) copy-start(bf16[3,128,128]{2,1,0:T(8,128)(2,1)} %copy-done.13) | copy-start | bytes 294916
  195.3 9.4 %all-to-all-start.8 = ((f32[4,128,128]{1,2,0:T(8,128)}), f32[4,128,128]{1,2,0:T(8,128)S(1)}, u32[]{:S(2)}, u32[]{:S(2)}) async-start(f32[4,128,128]{1,2,0:T(8,128)} %bitcast.182), calls=%async_computation.8 | async-start | bytes 524288 | tf_op jit(solution)/shard_map/all_to_all | solution.py:20
  198.7 10.8 %copy-start.15 = (bf16[3,128,128]{2,1,0:T(8,128)(2,1)}, bf16[3,128,128]{2,1,0:T(8,128)(2,1)S(1)}, u32[]{:S(2)}) copy-start(bf16[3,128,128]{2,1,0:T(8,128)(2,1)S(1)} %fusion.44) | copy-start | bytes 294916
  206.0 0.6 copy-start.7
  238.8 9.8 %all-to-all-start.12 = ((bf16[4,128,128]{2,1,0:T(8,128)(2,1)}), bf16[4,128,128]{2,1,0:T(8,128)(2,1)}, u32[]{:S(2)}, u32[]{:S(2)}) async-start(bf16[4,128,128]{2,1,0:T(8,128)(2,1)} %stack.18), calls=%async_computation.12 | async-start | bytes 262144 | tf_op jit(solution)/shard_map/all_to_all | solution.py:8
  242.9 9.1 %copy-start.8 = (f32[128,128]{1,0:T(8,128)S(1)}, f32[128,128]{1,0:T(8,128)}, u32[]{:S(2)}) copy-start(f32[128,128]{1,0:T(8,128)} %copy-done.7) | copy-start | bytes 196612
  242.9 9.1 %copy-start.16 = (bf16[3,128,128]{2,1,0:T(8,128)(2,1)S(1)}, bf16[3,128,128]{2,1,0:T(8,128)(2,1)}, u32[]{:S(2)}) copy-start(bf16[3,128,128]{2,1,0:T(8,128)(2,1)} %copy-done.15) | copy-start | bytes 294916
  248.6 9.4 %all-to-all-start.11 = ((f32[4,128,128]{1,2,0:T(8,128)}), f32[4,128,128]{1,2,0:T(8,128)S(1)}, u32[]{:S(2)}, u32[]{:S(2)}) async-start(f32[4,128,128]{1,2,0:T(8,128)} %bitcast.181), calls=%async_computation.11 | async-start | bytes 524288 | tf_op jit(solution)/shard_map/all_to_all | solution.py:20
  252.1 10.8 %copy-start.17 = (bf16[3,128,128]{2,1,0:T(8,128)(2,1)}, bf16[3,128,128]{2,1,0:T(8,128)(2,1)S(1)}, u32[]{:S(2)}) copy-start(bf16[3,128,128]{2,1,0:T(8,128)(2,1)S(1)} %fusion.43) | copy-start | bytes 294916
  259.3 0.6 copy-start.9
  292.2 9.8 %all-to-all-start.15 = ((bf16[4,128,128]{2,1,0:T(8,128)(2,1)}), bf16[4,128,128]{2,1,0:T(8,128)(2,1)}, u32[]{:S(2)}, u32[]{:S(2)}) async-start(bf16[4,128,128]{2,1,0:T(8,128)(2,1)} %stack.19), calls=%async_computation.15 | async-start | bytes 262144 | tf_op jit(solution)/shard_map/all_to_all | solution.py:8
  296.3 9.3 %copy-start.10 = (f32[128,128]{1,0:T(8,128)S(1)}, f32[128,128]{1,0:T(8,128)}, u32[]{:S(2)}) copy-start(f32[128,128]{1,0:T(8,128)} %copy-done.9) | copy-start | bytes 196612
  296.3 9.3 %copy-start.18 = (bf16[3,128,128]{2,1,0:T(8,128)(2,1)S(1)}, bf16[3,128,128]{2,1,0:T(8,128)(2,1)}, u32[]{:S(2)}) copy-start(bf16[3,128,128]{2,1,0:T(8,128)(2,1)} %copy-done.17) | copy-start | bytes 294916
  301.9 9.4 %all-to-all-start.14 = ((f32[4,128,128]{1,2,0:T(8,128)}), f32[4,128,128]{1,2,0:T(8,128)S(1)}, u32[]{:S(2)}, u32[]{:S(2)}) async-start(f32[4,128,128]{1,2,0:T(8,128)} %bitcast.180), calls=%async_computation.14 | async-start | bytes 524288 | tf_op jit(solution)/shard_map/all_to_all | solution.py:20
  312.7 0.6 copy-start.19
  345.5 9.8 %all-to-all-start.18 = ((bf16[4,128,128]{2,1,0:T(8,128)(2,1)}), bf16[4,128,128]{2,1,0:T(8,128)(2,1)}, u32[]{:S(2)}, u32[]{:S(2)}) async-start(bf16[4,128,128]{2,1,0:T(8,128)(2,1)} %stack.20), calls=%async_computation.18 | async-start | bytes 262144 | tf_op jit(solution)/shard_map/all_to_all | solution.py:8
  349.6 15.2 %copy-start.20 = (f32[128,128]{1,0:T(8,128)S(1)}, f32[128,128]{1,0:T(8,128)}, u32[]{:S(2)}) copy-start(f32[128,128]{1,0:T(8,128)} %copy-done.19) | copy-start | bytes 196612
  355.3 9.4 %all-to-all-start.17 = ((f32[4,128,128]{1,2,0:T(8,128)}), f32[4,128,128]{1,2,0:T(8,128)S(1)}, u32[]{:S(2)}, u32[]{:S(2)}) async-start(f32[4,128,128]{1,2,0:T(8,128)} %bitcast.179), calls=%async_computation.17 | async-start | bytes 524288 | tf_op jit(solution)/shard_map/all_to_all | solution.py:20
